TPU v7x, 256 devices: a whole 4x4x8 slice. The times are simulated.
256 devices in a mesh: blk: 8 (over y, x_hi), group: 32 (over z, x_lo, core).
Axes of the slice: x: 4 (x_hi: 2, x_lo: 2; x = x_hi * 2 + x_lo), y: 4, z: 8, core: 2. Of those that a mesh axis runs over, the one named last changes fastest.
Arguments:
- img_emb: bfloat16 [16384, 1152], P(('blk', 'group')), may hold values from -6 to 6
- txt_emb: bfloat16 [16384, 1152], P(('blk', 'group')), may hold values from -6 to 6
- img_ids: int32 [16384], P(('blk', 'group')), may hold values from 0 to 1023
- txt_ids: int32 [16384], P(('blk', 'group')), may hold values from 0 to 1023
- scale_logarithm: float32 [1], replicated, may hold values from 3.7 to 4.4
- bias: float32 [1], replicated, may hold values from -4 to -2
Outputs:
- img_grad: float32 [16384, 1152], P(('blk', 'group'))
- txt_grad: float32 [16384, 1152], P(('blk', 'group'))
All inputs are finite; a program needn't handle non-finite values.
Results may differ from a plain program's by a relative error of at most 0.0093.
Values may be sent and summed in bfloat16 or wider, within the bound.
A program may use at most 64 MiB of HBM per device.

v0:
```python
import functools

import jax
import jax.numpy as jnp
from jax import lax
from jax.experimental import pallas as pl
from jax.experimental.pallas import tpu as pltpu
from jax.sharding import PartitionSpec as P

MESH = pl.DeviceIdType.MESH
D = 1152
OWN = 64
HALF = 32
QUART = 16
ROWS = 1024
PIECE = 16
N_ARRIVALS = 134
N_SENT = 6

LINK_ROW, CORE_ROW, LINK_WAIT, CORE_WAIT, ISSUE, QUEUE = 0.0493, 0.0035, 2.0, 1.7, 0.03, 1.6

IMG_ORDER = [
    (4, 1), (4, 0),
    (3, 1), (5, 1), (3, 0), (5, 0),
    (2, 1), (6, 1), (2, 0), (6, 0),
    (1, 1), (7, 1), (0, 1), (1, 0), (7, 0), (0, 0),
]
IMG_ROW = {key: OWN * place for place, key in enumerate(IMG_ORDER)}

TXT_BASE = {
    ("A", 2): 0, ("B", 2): 128,
    ("A", 1): 256, ("A", 3): 384, ("B", 1): 512, ("B", 3): 640,
    ("A", 0): 768, ("B", 0): 896,
}


def txt_row(path, second, first):
    return TXT_BASE[path, second] + HALF * first


def unit_rows(embedding):
    widened = embedding.astype(jnp.float32)
    inverse = lax.rsqrt(jnp.sum(widened * widened, axis=1, keepdims=True) + 1e-06)
    return widened * inverse, inverse


class Plan:
    def __init__(self):
        self.steps, self.group_of, self.groups = {}, {}, {}

    def work(self, key, needs, cost, run):
        self.steps[key] = (tuple(needs), cost, run, None, 0.0)

    def copy(self, key, needs, rows, src, dst, to, group=None):
        length = rows * (CORE_ROW if to == "core" else LINK_ROW)
        self.steps[key] = (tuple(needs), length, (src, dst, to), to, CORE_WAIT if to == "core" else LINK_WAIT)
        self.group_of[key] = group or key
        self.groups.setdefault(group or key, []).append(key)

    def all_needs(self, key):
        result = []
        for need in self.steps[key][0]:
            result += self.groups[self.group_of[need]] if need in self.group_of else [need]
        return tuple(dict.fromkeys(result))

    def order(self):
        steps = {key: (self.all_needs(key), *step[1:]) for key, step in self.steps.items()}
        users = {key: [] for key in steps}
        for key, step in steps.items():
            for need in step[0]:
                users[need].append(key)
        left = {}

        def to_end(key):
            if key not in left:
                left[key] = steps[key][1] + steps[key][4] + max([to_end(user) for user in users[key]], default=0.0)
            return left[key]

        rank = {key: (-to_end(key), number) for number, key in enumerate(steps)}
        now, ready, free, end, result = 0.0, {}, {}, {}, []
        missing = {key: len(step[0]) for key, step in steps.items()}
        for key in steps:
            if not missing[key]:
                ready[key] = 0.0
        while ready:
            def opens(key):
                link = steps[key][3]
                return ready[key] if link is None else max(ready[key], free.get(link, 0.0) - QUEUE)

            now = max(now, min(opens(key) for key in ready))
            able = [key for key in ready if opens(key) <= now]
            key = min(able, key=lambda key: (steps[key][3] is None, rank[key]))
            del ready[key]
            needs, length, run, link, wait = steps[key]
            if link is None:
                now += length
                end[key] = now
            else:
                now += ISSUE
                free[link] = max(now, free.get(link, 0.0)) + length
                end[key] = free[link] + wait
            result.append(key)
            for user in users[key]:
                missing[user] -= 1
                if not missing[user]:
                    ready[user] = max(end[need] for need in steps[user][0])
        return result, end


def kernel(
    img_in, txt_in, img_ids_in, txt_ids_in, scale_in, bias_in, img_out, txt_out,
    img_ref, txt_ref, img_ids_ref, txt_ids_ref, scale_ref, bias_ref, in_sems,
    imgs, txts, img_ids, txt_ids, img_col, txt_line, coef, img_part, txt_part,
    t1_send, t1_recv, t2_send, t2_recv, t3_send, t3_recv, t4_send, t4_recv,
    core_send, core_recv, z_send, z_recv, send_sems, recv_sems,
):
    f32, bf16 = jnp.float32, jnp.bfloat16
    blk, grp = lax.axis_index("blk"), lax.axis_index("group")
    y, x_hi = lax.div(blk, 2), lax.rem(blk, 2)
    z, x_lo, core = lax.div(grp, 4), lax.rem(lax.div(grp, 2), 2), lax.rem(grp, 2)
    x = x_hi * 2 + x_lo

    def device(dx=0, dy=0, dz=0, dc=0):
        nx, ny, nz = lax.rem(x + dx + 4, 4), lax.rem(y + dy + 4, 4), lax.rem(z + dz + 8, 8)
        nc = lax.rem(core + dc, 2)
        return (ny * 2 + lax.div(nx, 2), (nz * 2 + lax.rem(nx, 2)) * 2 + nc)

    near = {
        "x+": device(dx=1), "x-": device(dx=-1), "y+": device(dy=1), "y-": device(dy=-1),
        "z+": device(dz=1), "z-": device(dz=-1), "core": device(dc=1),
    }
    barrier = pltpu.get_barrier_semaphore()
    for there in near.values():
        pl.semaphore_signal(barrier, inc=1, device_id=there, device_id_type=MESH)

    loads = [
        pltpu.make_async_copy(src, dst, in_sems.at[number])
        for number, (src, dst) in enumerate([
            (img_in, img_ref), (txt_in, txt_ref), (img_ids_in, img_ids_ref), (txt_ids_in, txt_ids_ref),
            (scale_in, scale_ref), (bias_in, bias_ref),
        ])
    ]
    for load in loads:
        load.start()
    for load in loads:
        load.wait()
    own_img, own_txt = IMG_ROW[0, 0], {p: txt_row(p, 0, 0) for p in "AB"}
    imgs[own_img:own_img + OWN, :] = unit_rows(img_ref[...])[0].astype(bf16)
    unit = unit_rows(txt_ref[...])[0].astype(bf16)
    txts[own_txt["A"]:own_txt["A"] + HALF, :] = unit[:HALF]
    txts[own_txt["B"]:own_txt["B"] + HALF, :] = unit[HALF:]
    line = img_ids_ref[...]
    img_ids[own_img // OWN] = jnp.concatenate([line] * 2, axis=1)
    line = txt_ids_ref[...]
    txt_ids[own_txt["A"] // HALF] = jnp.concatenate([line[:, :HALF]] * 4, axis=1)
    txt_ids[own_txt["B"] // HALF] = jnp.concatenate([line[:, HALF:]] * 4, axis=1)
    scale = jnp.exp(jnp.broadcast_to(scale_ref[...], (1, 256)))
    half_scale, half_bias = 0.5 * scale, 0.5 * jnp.broadcast_to(bias_ref[...], (1, 256))
    pl.semaphore_wait(barrier, len(near))

    plan = Plan()
    first_axis, second_axis = {"A": "x", "B": "y"}, {"A": "y", "B": "x"}
    halves = (0, 1)

    def move_text(p, src, dst, piece, to, needs):
        low = piece * QUART
        a, b = txt_row(p, *src) + low, txt_row(p, *dst) + low
        d, e = dst
        group = ("t", p, d) if d == 2 or (d == 1 and e > 1) or (d == 3 and e < 2) else None
        plan.copy(("t", p, *dst, piece), needs, QUART, txts.at[a:a + QUART, :], txts.at[b:b + QUART, :], to, group)

    def move_text_ids(p, src, dst, count, to, needs):
        a, b = txt_row(p, *src) // HALF, txt_row(p, *dst) // HALF
        group = ("ti", p, dst[0]) if dst in ((0, 2), (0, 3), (2, 0), (2, 2)) else None
        plan.copy(("ti", p, *dst), needs, 1, txt_ids.at[a:a + count], txt_ids.at[b:b + count], to, group)

    def text_here(p, d, e, piece):
        return [] if (d, e) == (0, 0) else [("t", p, d, e, piece)]

    for p in "AB":
        one, two = first_axis[p], second_axis[p]
        for e, way, order in ((1, "+", (0, 1)), (3, "-", (1, 0))):
            for piece in order:
                move_text(p, (0, 0), (0, e), piece, one + way, [])
        move_text(p, (0, 1), (0, 2), 0, one + "+", [("t", p, 0, 1, 0)])
        move_text(p, (0, 3), (0, 2), 1, one + "-", [("t", p, 0, 3, 1)])
        for e in range(4):
            for piece in halves:
                for d, way in ((1, "+"), (3, "-")):
                    move_text(p, (0, e), (d, e), piece, two + way, text_here(p, 0, e, piece))
                d, way = (1, "+") if e < 2 else (3, "-")
                move_text(p, (d, e), (2, e), piece, two + way, [("t", p, d, e, piece)])
        move_text_ids(p, (0, 0), (0, 1), 1, one + "+", [])
        move_text_ids(p, (0, 0), (0, 3), 1, one + "-", [])
        move_text_ids(p, (0, 1), (0, 2), 1, one + "+", [("ti", p, 0, 1)])
        line_ids = [("ti", p, 0, e) for e in (1, 2, 3)]
        move_text_ids(p, (0, 0), (1, 0), 4, two + "+", line_ids)
        move_text_ids(p, (0, 0), (3, 0), 4, two + "-", line_ids)
        move_text_ids(p, (1, 0), (2, 0), 2, two + "+", [("ti", p, 1, 0)])
        move_text_ids(p, (3, 2), (2, 2), 2, two + "-", [("ti", p, 3, 0)])

    pieces = [(low, low + PIECE) for low in range(0, OWN, PIECE)]

    def move_image(src, dst, low, high, to, needs):
        a, b = IMG_ROW[src, 0], IMG_ROW[dst, 0]
        group = ("z", 4, "half", low // HALF) if dst == 4 else None
        plan.copy(
            ("z", dst, low), needs, high - low, imgs.at[a + low:a + high, :], imgs.at[b + low:b + high, :], to, group
        )

    for way, step in (("+", 1), ("-", -1)):
        for hops in range(1, 5):
            src, dst = (hops - 1) * step % 8, hops * step % 8
            for low, high in pieces[::step]:
                if hops < 4 or (low < HALF) == (step > 0):
                    move_image(src, dst, low, high, "z" + way, [("z", src, low)] if src else [])
            if hops < 4 or step > 0:
                plan.copy(
                    ("zi", dst), [("zi", src)] if src else [], 1,
                    img_ids.at[IMG_ROW[src, 0] // OWN], img_ids.at[IMG_ROW[dst, 0] // OWN], "z" + way,
                )
    for dz in range(8):
        a, b = IMG_ROW[dz, 0], IMG_ROW[dz, 1]
        pair = min(dz, 8 - dz) or 1
        for half in halves:
            low, high = half * HALF, half * HALF + HALF
            plan.copy(
                ("c", dz, half), [("z", dz, at) for at, _ in pieces if low <= at < high and dz], HALF,
                imgs.at[a + low:a + high, :], imgs.at[b + low:b + high, :], "core", ("c", pair),
            )
        plan.copy(
            ("ci", dz), [("zi", dz)] if dz else [], 1, img_ids.at[a // OWN], img_ids.at[b // OWN], "core",
            ("ci", pair),
        )

    lane = lax.broadcasted_iota(jnp.int32, (1, 128), 1)

    def line_of_text(base):
        line = None
        for e in range(4):
            ids = txt_ids[base // HALF + e]
            line = ids if line is None else jnp.where(lane < HALF * e, line, ids)
        txt_line[:, base:base + 128] = line

    for (p, d), base in TXT_BASE.items():
        ids = {0: [("ti", p, 0, e) for e in (1, 2, 3)], 2: [("ti", p, 2, 0), ("ti", p, 2, 2)]}.get(d, [("ti", p, d, 0)])
        plan.work(("line", base), ids, 0.05, functools.partial(line_of_text, base))

    def column_of_images(row):
        place = row // OWN
        line = jnp.where(lane < OWN, img_ids[place], img_ids[place + 1])
        img_col[row:row + 128, :] = jnp.transpose(jnp.broadcast_to(line, (128, 128)))

    for row in range(0, ROWS, 128):
        ids = []
        for dz, cr in IMG_ORDER[row // OWN:row // OWN + 2]:
            ids += [("ci", dz)] if cr else [("zi", dz)] if dz else []
        plan.work(("column", row), ids, 0.1, functools.partial(column_of_images, row))

    def score_tile(r, rows, t):
        scores = lax.dot_general(
            imgs[r:r + rows, :], txts[t:t + 256, :], (((1,), (1,)), ((), ())), preferred_element_type=f32
        )
        column = img_col[r:r + rows, :]
        same = jnp.concatenate([column, column], axis=1) == txt_line[:, t:t + 256]
        value = 0.5 * jnp.tanh(half_scale * scores + half_bias) + jnp.where(same, -0.5, 0.5)
        coef[r:r + rows, t:t + 256] = value.astype(bf16)

    score_keys = []
    for t, cuts in ((768, (640, 384, 128, 0)), (256, (384, 128, 0)), (512, (384, 128, 0)), (0, (128, 0))):
        high = ROWS
        for r in cuts:
            needs = [("column", row) for row in range(r, high, 128)] + [("line", t), ("line", t + 128)]
            for dz, cr in IMG_ORDER[r // OWN:high // OWN]:
                needs += [("c", dz, half) for half in halves] if cr else [("z", dz, at) for at, _ in pieces if dz]
            for (p, d), base in TXT_BASE.items():
                if t <= base < t + 256:
                    needs += [at for e in range(4) for piece in halves for at in text_here(p, d, e, piece)]
            key = ("score", r, high, t)
            score_keys.append(key)
            plan.work(key, needs, 0.25 + 0.00056 * (high - r), functools.partial(score_tile, r, high - r, t))
            high = r

    def img_terms(row):
        img_part[row:row + 128, :] = jnp.dot(coef[row:row + 128, :], txts[...], preferred_element_type=f32)

    def txt_terms(row):
        txt_part[row:row + 128, :] = lax.dot_general(
            coef[:, row:row + 128], imgs[...], (((0,), (0,)), ((), ())), preferred_element_type=f32
        )

    for row in range(0, ROWS, 128):
        needs = [key for key in score_keys if key[1] <= row < key[2]]
        plan.work(("img", row), needs, 0.37, functools.partial(img_terms, row))
        needs = [key for key in score_keys if key[3] <= row < key[3] + 256]
        plan.work(("txt", row), needs, 0.38, functools.partial(txt_terms, row))

    def img_key(dz, cr):
        return ("img", IMG_ROW[dz, cr] // 128 * 128)

    def to_core(dz):
        row = IMG_ROW[dz, 1]
        core_send[OWN * dz:OWN * dz + OWN, :] = img_part[row:row + OWN, :].astype(bf16)

    def chip_sum(dz, low, high):
        row = IMG_ROW[dz, 0]
        return img_part[row + low:row + high, :] + core_recv[OWN * dz + low:OWN * dz + high, :].astype(f32)

    def z_out(dz, low, high, before):
        total = chip_sum(dz, low, high)
        if before:
            total = total + z_recv[OWN * before + low:OWN * before + high, :].astype(f32)
        z_send[OWN * dz + low:OWN * dz + high, :] = total.astype(bf16)

    for dz in range(8):
        rows = slice(OWN * dz, OWN * dz + OWN)
        plan.work(("to core", dz), [img_key(dz, 1)], 0.12, functools.partial(to_core, dz))
        plan.copy(("s", dz), [("to core", dz)], OWN, core_send.at[rows], core_recv.at[rows], "core", ("s", min(dz, 8 - dz)))
    for dz in (4, 3, 5, 2, 6, 1, 7):
        for low, high in pieces:
            if dz == 4:
                way, before = ("-" if low < HALF else "+"), 0
            else:
                way, before = ("-", dz + 1) if dz < 4 else ("+", dz - 1)
                if before == 4 and (low < HALF) != (way == "-"):
                    before = 0
            needs = [img_key(dz, 0), ("s", dz)] + ([("r", before, low)] if before else [])
            plan.work(("z out", dz, low), needs, 0.08, functools.partial(z_out, dz, low, high, before))
            rows = slice(OWN * dz + low, OWN * dz + high)
            plan.copy(
                ("r", dz, low), [("z out", dz, low)], high - low, z_send.at[rows], z_recv.at[rows], "z" + way,
                ("r", 1, "half", low // HALF) if dz in (1, 7) else None,
            )

    def t1_out(p, e):
        base, at = txt_row(p, 2, e), 128 * "AB".index(p) + HALF * e
        t1_send[at:at + HALF, :] = txt_part[base:base + HALF, :].astype(bf16)

    def t2_out(p, d, e, added):
        base, at = txt_row(p, d, e), 256 * "AB".index(p) + 128 * (d // 2) + HALF * e
        total = txt_part[base:base + HALF, :]
        if added:
            got = 128 * "AB".index(p) + HALF * e
            total = total + t1_recv[got:got + HALF, :].astype(f32)
        t2_send[at:at + HALF, :] = total.astype(bf16)

    def line_sum(p, e, low=0, high=HALF):
        base, at = txt_row(p, 0, e), 256 * "AB".index(p) + HALF * e
        return (
            txt_part[base + low:base + high, :]
            + t2_recv[at + low:at + high, :].astype(f32)
            + t2_recv[at + 128 + low:at + 128 + high, :].astype(f32)
        )

    def t3_out(p, part):
        at = HALF * "AB".index(p) + QUART * part
        t3_send[at:at + QUART, :] = line_sum(p, 2, QUART * part, QUART * part + QUART).astype(bf16)

    def t4_out(p, side, part):
        at = OWN * "AB".index(p) + HALF * side + QUART * part
        total = line_sum(p, 1 + 2 * side, QUART * part, QUART * part + QUART)
        if part == side:
            got = HALF * "AB".index(p) + QUART * part
            total = total + t3_recv[got:got + QUART, :].astype(f32)
        t4_send[at:at + QUART, :] = total.astype(bf16)

    def line_needs(p, e):
        return [("txt", TXT_BASE[p, 0]), ("t2", p, 1, e), ("t2", p, 3, e)]

    for p in "AB":
        one, two = first_axis[p], second_axis[p]
        for e in range(4):
            at = 128 * "AB".index(p) + HALF * e
            plan.work(("t1 out", p, e), [("txt", TXT_BASE[p, 2])], 0.1, functools.partial(t1_out, p, e))
            plan.copy(
                ("t1", p, e), [("t1 out", p, e)], HALF, t1_send.at[at:at + HALF], t1_recv.at[at:at + HALF],
                two + ("-" if e < 2 else "+"),
            )
            for d, way in ((1, "-"), (3, "+")):
                added = (d == 1) == (e < 2)
                at = 256 * "AB".index(p) + 128 * (d // 2) + HALF * e
                needs = [("txt", TXT_BASE[p, d])] + ([("t1", p, e)] if added else [])
                plan.work(("t2 out", p, d, e), needs, 0.12, functools.partial(t2_out, p, d, e, added))
                plan.copy(
                    ("t2", p, d, e), [("t2 out", p, d, e)], HALF, t2_send.at[at:at + HALF], t2_recv.at[at:at + HALF],
                    two + way, ("t2", p, e),
                )
        for part, way in ((0, "-"), (1, "+")):
            at = HALF * "AB".index(p) + QUART * part
            plan.work(("t3 out", p, part), line_needs(p, 2), 0.08, functools.partial(t3_out, p, part))
            plan.copy(
                ("t3", p, part), [("t3 out", p, part)], QUART, t3_send.at[at:at + QUART], t3_recv.at[at:at + QUART],
                one + way,
            )
        for side, way in ((0, "-"), (1, "+")):
            for part in halves:
                at = OWN * "AB".index(p) + HALF * side + QUART * part
                needs = line_needs(p, 1 + 2 * side) + ([("t3", p, part)] if part == side else [])
                plan.work(("t4 out", p, side, part), needs, 0.08, functools.partial(t4_out, p, side, part))
                plan.copy(
                    ("t4", p, side, part), [("t4 out", p, side, part)], QUART,
                    t4_send.at[at:at + QUART], t4_recv.at[at:at + QUART], one + way, ("t4", p),
                )

    def finish(embedding, total):
        unit, inverse = unit_rows(embedding)
        direction = scale[:, 0:1] * total
        return inverse * (direction - unit * jnp.sum(unit * direction, axis=1, keepdims=True))

    def finish_txt(p):
        low = HALF * "AB".index(p)
        total = line_sum(p, 0)
        for side in halves:
            at = OWN * "AB".index(p) + HALF * side
            total = total + t4_recv[at:at + HALF, :].astype(f32)
        txt_out[low:low + HALF, :] = finish(txt_ref[low:low + HALF, :], total)

    def finish_img(low, high):
        total = chip_sum(0, low, high)
        for dz in (1, 7):
            total = total + z_recv[OWN * dz + low:OWN * dz + high, :].astype(f32)
        img_out[low:high, :] = finish(img_ref[low:high, :], total)

    for p in "AB":
        needs = line_needs(p, 0) + [("t4", p, side, part) for side in halves for part in halves]
        plan.work(("end", p), needs, 0.2, functools.partial(finish_txt, p))
    for low in (HALF, 0):
        needs = [img_key(0, 0), ("s", 0), ("r", 1, low)]
        plan.work(("end", low), needs, 0.15, functools.partial(finish_img, low, low + HALF))

    arrives = {group: recv_sems.at[number] for number, group in enumerate(plan.groups)}
    sent = []

    def whole(rows, ids):
        return txt_ids.at[0:rows] if ids else imgs.at[0:rows, :]

    def await_copy(ref, sem):
        pltpu.make_async_copy(ref, ref, sem).wait()

    here = set()
    for key in plan.order()[0]:
        needs, _, run, link, _ = plan.steps[key]
        for need in needs:
            group = plan.group_of.get(need)
            if group is None or group in here:
                continue
            here.add(group)
            landed = [plan.steps[member][2][1] for member in plan.groups[group]]
            ids = landed[0].dtype != bf16
            await_copy(whole(sum(1 if ref.ndim == 2 and ids else ref.shape[0] for ref in landed), ids), arrives[group])
        if link is None:
            run()
            continue
        src, dst, to = run
        ids = src.dtype != bf16
        rows = 1 if src.ndim == 2 and ids else src.shape[0]
        open_sems = [entry for entry in sent if entry[0] == ids and entry[1] + rows <= (32 if ids else ROWS)]
        if not open_sems:
            open_sems = [[ids, 0, send_sems.at[len(sent)]]]
            sent.append(open_sems[0])
        open_sems[0][1] += rows
        pltpu.make_async_remote_copy(
            src_ref=src, dst_ref=dst, send_sem=open_sems[0][2], recv_sem=arrives[plan.group_of[key]],
            device_id=near[to], device_id_type=MESH,
        ).start()
    for ids, rows, sem in sent:
        await_copy(whole(rows, ids), sem)


def write_out(img_grad, txt_grad, img_out, txt_out, sems):
    copies = [
        pltpu.make_async_copy(src, dst, sems.at[number])
        for number, (src, dst) in enumerate([(img_grad, img_out), (txt_grad, txt_out)])
    ]
    for copy in copies:
        copy.start()
    for copy in copies:
        copy.wait()


def body(img_emb, txt_emb, img_ids, txt_ids, scale_logarithm, bias):
    f32, bf16, i32 = jnp.float32, jnp.bfloat16, jnp.int32
    anywhere = pl.BlockSpec(memory_space=pl.ANY)
    in_vmem = pl.BlockSpec(memory_space=pltpu.VMEM)
    grads = pl.pallas_call(
        kernel,
        out_shape=(pltpu.VMEM((OWN, D), f32), pltpu.VMEM((OWN, D), f32)),
        in_specs=[anywhere] * 6,
        out_specs=(in_vmem, in_vmem),
        scratch_shapes=[
            pltpu.VMEM((OWN, D), bf16),
            pltpu.VMEM((OWN, D), bf16),
            pltpu.VMEM((1, OWN), i32),
            pltpu.VMEM((1, OWN), i32),
            pltpu.VMEM((1, 1), f32),
            pltpu.VMEM((1, 1), f32),
            pltpu.SemaphoreType.DMA((6,)),
            pltpu.VMEM((ROWS, D), bf16),
            pltpu.VMEM((ROWS, D), bf16),
            pltpu.VMEM((16, 1, 128), i32),
            pltpu.VMEM((32, 1, 128), i32),
            pltpu.VMEM((ROWS, 128), i32),
            pltpu.VMEM((1, ROWS), i32),
            pltpu.VMEM((ROWS, ROWS), bf16),
            pltpu.VMEM((ROWS, D), f32),
            pltpu.VMEM((ROWS, D), f32),
            pltpu.VMEM((256, D), bf16),
            pltpu.VMEM((256, D), bf16),
            pltpu.VMEM((512, D), bf16),
            pltpu.VMEM((512, D), bf16),
            pltpu.VMEM((64, D), bf16),
            pltpu.VMEM((64, D), bf16),
            pltpu.VMEM((128, D), bf16),
            pltpu.VMEM((128, D), bf16),
            pltpu.VMEM((512, D), bf16),
            pltpu.VMEM((512, D), bf16),
            pltpu.VMEM((512, D), bf16),
            pltpu.VMEM((512, D), bf16),
            pltpu.SemaphoreType.DMA((N_SENT,)),
            pltpu.SemaphoreType.DMA((N_ARRIVALS,)),
        ],
        compiler_params=pltpu.CompilerParams(
            collective_id=0, has_side_effects=True, vmem_limit_bytes=56 * 1024 * 1024
        ),
        cost_estimate=pl.CostEstimate(flops=7247757312, bytes_accessed=900000, transcendentals=1048576),
    )(img_emb, txt_emb, img_ids.reshape(1, OWN), txt_ids.reshape(1, OWN),
      scale_logarithm.reshape(1, 1), bias.reshape(1, 1))
    return pl.pallas_call(
        write_out,
        out_shape=(jax.ShapeDtypeStruct((OWN, D), f32), jax.ShapeDtypeStruct((OWN, D), f32)),
        in_specs=[in_vmem, in_vmem],
        out_specs=(anywhere, anywhere),
        scratch_shapes=[pltpu.SemaphoreType.DMA((2,))],
    )(*[pltpu.with_memory_space_constraint(grad, pltpu.VMEM) for grad in grads])


def solution(mesh):
    split = P(("blk", "group"), None)
    ids = P(("blk", "group"))
    return jax.shard_map(
        body,
        mesh=mesh,
        in_specs=(split, split, ids, ids, P(), P()),
        out_specs=(split, split),
        check_vma=False,
    )
```

profile of v0, /device:TPU:1, one launch (start us, length us, event | category | flops | bytes accessed | tf_op | source)
XLA Modules:
  0.0 51.9 jit_solution(17605042974228500964)
XLA Ops:
  1.9 49.1 %shard_map.77 = (f32[64,1152]{1,0:T(8,128)S(1)}, f32[64,1152]{1,0:T(8,128)S(1)}) custom-call(bf16[64,1152]{1,0:T(8,128)(2,1)} %img_in.1, bf16[64,1152]{1,0:T(8,128)(2,1)} %txt_in.1, s32[1,64]{1,0:T(1,128)} %bitcast.6, s32[1,64]{1,0:T(1,128)} %bitcast.7, f32[1,1]{1,0:T(1,128)} %bitcast.4.scale_in, f32[1,1]{1,0:T(1,128)} %bitcast.5.bias_in), custom_call_target="tpu_custom_call" | custom-call | flops 7247757312 | bytes 900000 | tf_op jit(solution)/shard_map/pallas_call | solution.py:485
  51.1 0.8 %shard_map.78 = (f32[64,1152]{1,0:T(8,128)}, f32[64,1152]{1,0:T(8,128)}) custom-call(f32[64,1152]{1,0:T(8,128)S(1)} %get-tuple-element.4.img_grad, f32[64,1152]{1,0:T(8,128)S(1)} %get-tuple-element.5.txt_grad), custom_call_target="tpu_custom_call" | custom-call | tf_op jit(solution)/shard_map/pallas_call | solution.py:528
where the time goes:
time: 52.2 us; the launch traced here: 51.9 us
  Pallas kernels  50 us (96%)
  between operations  1.93 us (4%)
    pallas_call x1, Pallas kernels, body(): pl.pallas_call(kernel, out_shape=(pltpu.VMEM((OWN, D), f32), pltpu.VMEM((...  49.1 us

commit v1 on v0

--- a/solution.py
+++ b/solution.py
@@ -14,10 +14,14 @@
 QUART = 16
 ROWS = 1024
 PIECE = 16
-N_ARRIVALS = 134
+N_ARRIVALS = 146
 N_SENT = 6
 
-LINK_ROW, CORE_ROW, LINK_WAIT, CORE_WAIT, ISSUE, QUEUE = 0.0493, 0.0035, 2.0, 1.7, 0.03, 1.6
+LINK_ROW, CORE_ROW, LINK_WAIT, CORE_WAIT, ISSUE, QUEUE = 0.0493, 0.0035, 2.2, 1.7, 0.03, 1.6
+ROUTE = {
+    **{way: ((way,), 1, 0.0) for way in ("x+", "x-", "y+", "y-", "z+", "z-", "core")},
+    "x2": (("x+", "x-"), 1, 0.6), "y2": (("y+", "y-"), 1, 0.6), "z+2": (("z+",), 2, 0.6), "z-2": (("z-",), 2, 0.6),
+}
 
 IMG_ORDER = [
     (4, 1), (4, 0),
@@ -27,15 +31,22 @@
 ]
 IMG_ROW = {key: OWN * place for place, key in enumerate(IMG_ORDER)}
 
-TXT_BASE = {
-    ("A", 2): 0, ("B", 2): 128,
-    ("A", 1): 256, ("A", 3): 384, ("B", 1): 512, ("B", 3): 640,
-    ("A", 0): 768, ("B", 0): 896,
-}
-
-
-def txt_row(path, second, first):
-    return TXT_BASE[path, second] + HALF * first
+TXT_ORDER = (
+    [(p, 2, e) for p in "AB" for e in range(4)]
+    + [(p, d, e) for p in "AB" for d, e in ((1, 2), (1, 3), (3, 0), (3, 1))]
+    + [(p, d, e) for p in "AB" for d, e in ((1, 0), (1, 1), (3, 2), (3, 3))]
+    + [(p, 0, e) for p in "AB" for e in range(4)]
+)
+TXT_ROW = {key: HALF * place for place, key in enumerate(TXT_ORDER)}
+
+
+SCORE_TILES = [
+    (640, 1024, 768, 1024), (384, 640, 768, 1024), (128, 384, 768, 1024),
+    (384, 1024, 512, 768), (128, 384, 512, 768),
+    (384, 1024, 256, 512), (128, 384, 256, 512),
+    (128, 1024, 0, 256),
+    (0, 128, 0, 1024),
+]
 
 
 def unit_rows(embedding):
@@ -52,8 +63,10 @@
         self.steps[key] = (tuple(needs), cost, run, None, 0.0)
 
     def copy(self, key, needs, rows, src, dst, to, group=None):
-        length = rows * (CORE_ROW if to == "core" else LINK_ROW)
-        self.steps[key] = (tuple(needs), length, (src, dst, to), to, CORE_WAIT if to == "core" else LINK_WAIT)
+        links, times, more = ROUTE[to]
+        length = rows * times * (CORE_ROW if to == "core" else LINK_ROW)
+        wait = CORE_WAIT if to == "core" else LINK_WAIT + more
+        self.steps[key] = (tuple(needs), length, (src, dst, to), links, wait)
         self.group_of[key] = group or key
         self.groups.setdefault(group or key, []).append(key)
 
@@ -84,21 +97,22 @@
                 ready[key] = 0.0
         while ready:
             def opens(key):
-                link = steps[key][3]
-                return ready[key] if link is None else max(ready[key], free.get(link, 0.0) - QUEUE)
+                links = steps[key][3] or ()
+                return max([ready[key]] + [free.get(link, 0.0) - QUEUE for link in links])
 
             now = max(now, min(opens(key) for key in ready))
             able = [key for key in ready if opens(key) <= now]
             key = min(able, key=lambda key: (steps[key][3] is None, rank[key]))
             del ready[key]
-            needs, length, run, link, wait = steps[key]
-            if link is None:
+            needs, length, run, links, wait = steps[key]
+            if links is None:
                 now += length
                 end[key] = now
             else:
                 now += ISSUE
-                free[link] = max(now, free.get(link, 0.0)) + length
-                end[key] = free[link] + wait
+                for link in links:
+                    free[link] = max(now, free.get(link, 0.0)) + length
+                end[key] = max(free[link] for link in links) + wait
             result.append(key)
             for user in users[key]:
                 missing[user] -= 1
@@ -111,7 +125,7 @@
     img_in, txt_in, img_ids_in, txt_ids_in, scale_in, bias_in, img_out, txt_out,
     img_ref, txt_ref, img_ids_ref, txt_ids_ref, scale_ref, bias_ref, in_sems,
     imgs, txts, img_ids, txt_ids, img_col, txt_line, coef, img_part, txt_part,
-    t1_send, t1_recv, t2_send, t2_recv, t3_send, t3_recv, t4_send, t4_recv,
+    t1_send, t1_recv, t2_send, t2_recv, t3_send, t3_recv,
     core_send, core_recv, z_send, z_recv, send_sems, recv_sems,
 ):
     f32, bf16 = jnp.float32, jnp.bfloat16
@@ -128,6 +142,7 @@
     near = {
         "x+": device(dx=1), "x-": device(dx=-1), "y+": device(dy=1), "y-": device(dy=-1),
         "z+": device(dz=1), "z-": device(dz=-1), "core": device(dc=1),
+        "x2": device(dx=2), "y2": device(dy=2), "z+2": device(dz=2), "z-2": device(dz=-2),
     }
     barrier = pltpu.get_barrier_semaphore()
     for there in near.values():
@@ -144,7 +159,7 @@
         load.start()
     for load in loads:
         load.wait()
-    own_img, own_txt = IMG_ROW[0, 0], {p: txt_row(p, 0, 0) for p in "AB"}
+    own_img, own_txt = IMG_ROW[0, 0], {p: TXT_ROW[p, 0, 0] for p in "AB"}
     imgs[own_img:own_img + OWN, :] = unit_rows(img_ref[...])[0].astype(bf16)
     unit = unit_rows(txt_ref[...])[0].astype(bf16)
     txts[own_txt["A"]:own_txt["A"] + HALF, :] = unit[:HALF]
@@ -155,7 +170,7 @@
     txt_ids[own_txt["A"] // HALF] = jnp.concatenate([line[:, :HALF]] * 4, axis=1)
     txt_ids[own_txt["B"] // HALF] = jnp.concatenate([line[:, HALF:]] * 4, axis=1)
     scale = jnp.exp(jnp.broadcast_to(scale_ref[...], (1, 256)))
-    half_scale, half_bias = 0.5 * scale, 0.5 * jnp.broadcast_to(bias_ref[...], (1, 256))
+    half_scale, half_bias = 0.5 * scale[:, 0:1], 0.5 * bias_ref[...]
     pl.semaphore_wait(barrier, len(near))
 
     plan = Plan()
@@ -164,14 +179,17 @@
 
     def move_text(p, src, dst, piece, to, needs):
         low = piece * QUART
-        a, b = txt_row(p, *src) + low, txt_row(p, *dst) + low
+        a, b = TXT_ROW[p, *src] + low, TXT_ROW[p, *dst] + low
         d, e = dst
-        group = ("t", p, d) if d == 2 or (d == 1 and e > 1) or (d == 3 and e < 2) else None
+        group = ("t", p, "far") if d == 2 else ("t", p, "rest") if (d == 1 and e > 1) or (d == 3 and e < 2) else None
         plan.copy(("t", p, *dst, piece), needs, QUART, txts.at[a:a + QUART, :], txts.at[b:b + QUART, :], to, group)
 
     def move_text_ids(p, src, dst, count, to, needs):
-        a, b = txt_row(p, *src) // HALF, txt_row(p, *dst) // HALF
-        group = ("ti", p, dst[0]) if dst in ((0, 2), (0, 3), (2, 0), (2, 2)) else None
+        a, b = TXT_ROW[p, *src] // HALF, TXT_ROW[p, *dst] // HALF
+        group = {
+            (0, 2): ("ti", p, 0), (0, 3): ("ti", p, 0), (2, 0): ("ti", p, 2), (2, 2): ("ti", p, 2),
+            (1, 2): ("ti", p, "rest"), (3, 0): ("ti", p, "rest"),
+        }.get(dst)
         plan.copy(("ti", p, *dst), needs, 1, txt_ids.at[a:a + count], txt_ids.at[b:b + count], to, group)
 
     def text_here(p, d, e, piece):
@@ -182,8 +200,8 @@
         for e, way, order in ((1, "+", (0, 1)), (3, "-", (1, 0))):
             for piece in order:
                 move_text(p, (0, 0), (0, e), piece, one + way, [])
-        move_text(p, (0, 1), (0, 2), 0, one + "+", [("t", p, 0, 1, 0)])
-        move_text(p, (0, 3), (0, 2), 1, one + "-", [("t", p, 0, 3, 1)])
+        for piece in halves:
+            move_text(p, (0, 0), (0, 2), piece, one + "2", [])
         for e in range(4):
             for piece in halves:
                 for d, way in ((1, "+"), (3, "-")):
@@ -192,12 +210,12 @@
                 move_text(p, (d, e), (2, e), piece, two + way, [("t", p, d, e, piece)])
         move_text_ids(p, (0, 0), (0, 1), 1, one + "+", [])
         move_text_ids(p, (0, 0), (0, 3), 1, one + "-", [])
-        move_text_ids(p, (0, 1), (0, 2), 1, one + "+", [("ti", p, 0, 1)])
-        line_ids = [("ti", p, 0, e) for e in (1, 2, 3)]
-        move_text_ids(p, (0, 0), (1, 0), 4, two + "+", line_ids)
-        move_text_ids(p, (0, 0), (3, 0), 4, two + "-", line_ids)
+        move_text_ids(p, (0, 0), (0, 2), 1, one + "2", [])
+        for d, way in ((1, "+"), (3, "-")):
+            move_text_ids(p, (0, 0), (d, 0), 2, two + way, [("ti", p, 0, 1)])
+            move_text_ids(p, (0, 2), (d, 2), 2, two + way, [("ti", p, 0, 2), ("ti", p, 0, 3)])
         move_text_ids(p, (1, 0), (2, 0), 2, two + "+", [("ti", p, 1, 0)])
-        move_text_ids(p, (3, 2), (2, 2), 2, two + "-", [("ti", p, 3, 0)])
+        move_text_ids(p, (3, 2), (2, 2), 2, two + "-", [("ti", p, 3, 2)])
 
     pieces = [(low, low + PIECE) for low in range(0, OWN, PIECE)]
 
@@ -210,14 +228,15 @@
 
     for way, step in (("+", 1), ("-", -1)):
         for hops in range(1, 5):
-            src, dst = (hops - 1) * step % 8, hops * step % 8
+            src, dst = (hops - 1 - hops // 4) * step % 8, hops * step % 8
+            to = "z" + way + ("2" if hops == 4 else "")
             for low, high in pieces[::step]:
                 if hops < 4 or (low < HALF) == (step > 0):
-                    move_image(src, dst, low, high, "z" + way, [("z", src, low)] if src else [])
+                    move_image(src, dst, low, high, to, [("z", src, low)] if src else [])
             if hops < 4 or step > 0:
                 plan.copy(
                     ("zi", dst), [("zi", src)] if src else [], 1,
-                    img_ids.at[IMG_ROW[src, 0] // OWN], img_ids.at[IMG_ROW[dst, 0] // OWN], "z" + way,
+                    img_ids.at[IMG_ROW[src, 0] // OWN], img_ids.at[IMG_ROW[dst, 0] // OWN], to,
                 )
     for dz in range(8):
         a, b = IMG_ROW[dz, 0], IMG_ROW[dz, 1]
@@ -242,8 +261,11 @@
             line = ids if line is None else jnp.where(lane < HALF * e, line, ids)
         txt_line[:, base:base + 128] = line
 
-    for (p, d), base in TXT_BASE.items():
-        ids = {0: [("ti", p, 0, e) for e in (1, 2, 3)], 2: [("ti", p, 2, 0), ("ti", p, 2, 2)]}.get(d, [("ti", p, d, 0)])
+    for base in range(0, ROWS, 128):
+        ids = []
+        for p, d, e in TXT_ORDER[base // HALF:base // HALF + 4]:
+            if (d, e) != (0, 0):
+                ids.append(("ti", p, d, e if d == 0 else e // 2 * 2))
         plan.work(("line", base), ids, 0.05, functools.partial(line_of_text, base))
 
     def column_of_images(row):
@@ -257,29 +279,26 @@
             ids += [("ci", dz)] if cr else [("zi", dz)] if dz else []
         plan.work(("column", row), ids, 0.1, functools.partial(column_of_images, row))
 
-    def score_tile(r, rows, t):
+    def score_tile(r, high, t, right):
         scores = lax.dot_general(
-            imgs[r:r + rows, :], txts[t:t + 256, :], (((1,), (1,)), ((), ())), preferred_element_type=f32
+            imgs[r:high, :], txts[t:right, :], (((1,), (1,)), ((), ())), preferred_element_type=f32
         )
-        column = img_col[r:r + rows, :]
-        same = jnp.concatenate([column, column], axis=1) == txt_line[:, t:t + 256]
+        column = img_col[r:high, :]
+        same = jnp.concatenate([column] * ((right - t) // 128), axis=1) == txt_line[:, t:right]
         value = 0.5 * jnp.tanh(half_scale * scores + half_bias) + jnp.where(same, -0.5, 0.5)
-        coef[r:r + rows, t:t + 256] = value.astype(bf16)
+        coef[r:high, t:right] = value.astype(bf16)
 
     score_keys = []
-    for t, cuts in ((768, (640, 384, 128, 0)), (256, (384, 128, 0)), (512, (384, 128, 0)), (0, (128, 0))):
-        high = ROWS
-        for r in cuts:
-            needs = [("column", row) for row in range(r, high, 128)] + [("line", t), ("line", t + 128)]
-            for dz, cr in IMG_ORDER[r // OWN:high // OWN]:
-                needs += [("c", dz, half) for half in halves] if cr else [("z", dz, at) for at, _ in pieces if dz]
-            for (p, d), base in TXT_BASE.items():
-                if t <= base < t + 256:
-                    needs += [at for e in range(4) for piece in halves for at in text_here(p, d, e, piece)]
-            key = ("score", r, high, t)
-            score_keys.append(key)
-            plan.work(key, needs, 0.25 + 0.00056 * (high - r), functools.partial(score_tile, r, high - r, t))
-            high = r
+    for r, high, t, right in SCORE_TILES:
+        needs = [("column", row) for row in range(r, high, 128)] + [("line", base) for base in range(t, right, 128)]
+        for dz, cr in IMG_ORDER[r // OWN:high // OWN]:
+            needs += [("c", dz, half) for half in halves] if cr else [("z", dz, at) for at, _ in pieces if dz]
+        for p, d, e in TXT_ORDER[t // HALF:right // HALF]:
+            needs += [at for piece in halves for at in text_here(p, d, e, piece)]
+        key = ("score", r, high, t, right)
+        score_keys.append(key)
+        cost = 0.12 + max(0.225, 0.00088 * (high - r)) * (right - t) / 256
+        plan.work(key, needs, cost, functools.partial(score_tile, r, high, t, right))
 
     def img_terms(row):
         img_part[row:row + 128, :] = jnp.dot(coef[row:row + 128, :], txts[...], preferred_element_type=f32)
@@ -292,7 +311,7 @@
     for row in range(0, ROWS, 128):
         needs = [key for key in score_keys if key[1] <= row < key[2]]
         plan.work(("img", row), needs, 0.37, functools.partial(img_terms, row))
-        needs = [key for key in score_keys if key[3] <= row < key[3] + 256]
+        needs = [key for key in score_keys if key[3] <= row < key[4]]
         plan.work(("txt", row), needs, 0.38, functools.partial(txt_terms, row))
 
     def img_key(dz, cr):
@@ -308,8 +327,8 @@
 
     def z_out(dz, low, high, before):
         total = chip_sum(dz, low, high)
-        if before:
-            total = total + z_recv[OWN * before + low:OWN * before + high, :].astype(f32)
+        for other in before:
+            total = total + z_recv[OWN * other + low:OWN * other + high, :].astype(f32)
         z_send[OWN * dz + low:OWN * dz + high, :] = total.astype(bf16)
 
     for dz in range(8):
@@ -318,89 +337,85 @@
         plan.copy(("s", dz), [("to core", dz)], OWN, core_send.at[rows], core_recv.at[rows], "core", ("s", min(dz, 8 - dz)))
     for dz in (4, 3, 5, 2, 6, 1, 7):
         for low, high in pieces:
-            if dz == 4:
-                way, before = ("-" if low < HALF else "+"), 0
-            else:
-                way, before = ("-", dz + 1) if dz < 4 else ("+", dz - 1)
-                if before == 4 and (low < HALF) != (way == "-"):
-                    before = 0
-            needs = [img_key(dz, 0), ("s", dz)] + ([("r", before, low)] if before else [])
+            way = "-" if dz < 4 or dz == 4 and low < HALF else "+"
+            before = []
+            if dz in (1, 2, 6, 7):
+                before.append(dz + 1 if dz < 4 else dz - 1)
+            if dz in (2, 6) and (low < HALF) == (dz == 2):
+                before.append(4)
+            needs = [img_key(dz, 0), ("s", dz)] + [("r", other, low) for other in before]
             plan.work(("z out", dz, low), needs, 0.08, functools.partial(z_out, dz, low, high, before))
             rows = slice(OWN * dz + low, OWN * dz + high)
             plan.copy(
-                ("r", dz, low), [("z out", dz, low)], high - low, z_send.at[rows], z_recv.at[rows], "z" + way,
+                ("r", dz, low), [("z out", dz, low)], high - low, z_send.at[rows], z_recv.at[rows],
+                "z" + way + ("2" if dz == 4 else ""),
                 ("r", 1, "half", low // HALF) if dz in (1, 7) else None,
             )
 
-    def t1_out(p, e):
-        base, at = txt_row(p, 2, e), 128 * "AB".index(p) + HALF * e
-        t1_send[at:at + HALF, :] = txt_part[base:base + HALF, :].astype(bf16)
-
-    def t2_out(p, d, e, added):
-        base, at = txt_row(p, d, e), 256 * "AB".index(p) + 128 * (d // 2) + HALF * e
-        total = txt_part[base:base + HALF, :]
+    def t1_out(p, e, low, high):
+        base, at = TXT_ROW[p, 2, e], 128 * "AB".index(p) + HALF * e
+        t1_send[at + low:at + high, :] = txt_part[base + low:base + high, :].astype(bf16)
+
+    def t2_out(p, d, e, low, high, added):
+        base, at = TXT_ROW[p, d, e], 256 * "AB".index(p) + 128 * (d // 2) + HALF * e
+        total = txt_part[base + low:base + high, :]
         if added:
             got = 128 * "AB".index(p) + HALF * e
-            total = total + t1_recv[got:got + HALF, :].astype(f32)
-        t2_send[at:at + HALF, :] = total.astype(bf16)
+            total = total + t1_recv[got + low:got + high, :].astype(f32)
+        t2_send[at + low:at + high, :] = total.astype(bf16)
 
     def line_sum(p, e, low=0, high=HALF):
-        base, at = txt_row(p, 0, e), 256 * "AB".index(p) + HALF * e
+        base, at = TXT_ROW[p, 0, e], 256 * "AB".index(p) + HALF * e
         return (
             txt_part[base + low:base + high, :]
             + t2_recv[at + low:at + high, :].astype(f32)
             + t2_recv[at + 128 + low:at + 128 + high, :].astype(f32)
         )
 
-    def t3_out(p, part):
-        at = HALF * "AB".index(p) + QUART * part
-        t3_send[at:at + QUART, :] = line_sum(p, 2, QUART * part, QUART * part + QUART).astype(bf16)
-
-    def t4_out(p, side, part):
-        at = OWN * "AB".index(p) + HALF * side + QUART * part
-        total = line_sum(p, 1 + 2 * side, QUART * part, QUART * part + QUART)
-        if part == side:
-            got = HALF * "AB".index(p) + QUART * part
-            total = total + t3_recv[got:got + QUART, :].astype(f32)
-        t4_send[at:at + QUART, :] = total.astype(bf16)
-
-    def line_needs(p, e):
-        return [("txt", TXT_BASE[p, 0]), ("t2", p, 1, e), ("t2", p, 3, e)]
+    def t3_out(p, e, low, high):
+        at = 96 * "AB".index(p) + HALF * (e - 1)
+        t3_send[at + low:at + high, :] = line_sum(p, e, low, high).astype(bf16)
+
+    def txt_key(p, d, e):
+        return ("txt", TXT_ROW[p, d, e] // 128 * 128)
+
+    def line_needs(p, e, low):
+        return [txt_key(p, 0, e), ("t2", p, 1, e, low), ("t2", p, 3, e, low)]
 
     for p in "AB":
         one, two = first_axis[p], second_axis[p]
         for e in range(4):
-            at = 128 * "AB".index(p) + HALF * e
-            plan.work(("t1 out", p, e), [("txt", TXT_BASE[p, 2])], 0.1, functools.partial(t1_out, p, e))
-            plan.copy(
-                ("t1", p, e), [("t1 out", p, e)], HALF, t1_send.at[at:at + HALF], t1_recv.at[at:at + HALF],
-                two + ("-" if e < 2 else "+"),
-            )
-            for d, way in ((1, "-"), (3, "+")):
-                added = (d == 1) == (e < 2)
-                at = 256 * "AB".index(p) + 128 * (d // 2) + HALF * e
-                needs = [("txt", TXT_BASE[p, d])] + ([("t1", p, e)] if added else [])
-                plan.work(("t2 out", p, d, e), needs, 0.12, functools.partial(t2_out, p, d, e, added))
+            for low in (0, QUART):
+                high = low + QUART
+                at = 128 * "AB".index(p) + HALF * e
+                rows = slice(at + low, at + high)
+                plan.work(("t1 out", p, e, low), [txt_key(p, 2, e)], 0.06, functools.partial(t1_out, p, e, low, high))
                 plan.copy(
-                    ("t2", p, d, e), [("t2 out", p, d, e)], HALF, t2_send.at[at:at + HALF], t2_recv.at[at:at + HALF],
-                    two + way, ("t2", p, e),
+                    ("t1", p, e, low), [("t1 out", p, e, low)], QUART, t1_send.at[rows], t1_recv.at[rows],
+                    two + ("-" if e < 2 else "+"),
                 )
-        for part, way in ((0, "-"), (1, "+")):
-            at = HALF * "AB".index(p) + QUART * part
-            plan.work(("t3 out", p, part), line_needs(p, 2), 0.08, functools.partial(t3_out, p, part))
-            plan.copy(
-                ("t3", p, part), [("t3 out", p, part)], QUART, t3_send.at[at:at + QUART], t3_recv.at[at:at + QUART],
-                one + way,
-            )
-        for side, way in ((0, "-"), (1, "+")):
-            for part in halves:
-                at = OWN * "AB".index(p) + HALF * side + QUART * part
-                needs = line_needs(p, 1 + 2 * side) + ([("t3", p, part)] if part == side else [])
-                plan.work(("t4 out", p, side, part), needs, 0.08, functools.partial(t4_out, p, side, part))
-                plan.copy(
-                    ("t4", p, side, part), [("t4 out", p, side, part)], QUART,
-                    t4_send.at[at:at + QUART], t4_recv.at[at:at + QUART], one + way, ("t4", p),
-                )
+                for d, way in ((1, "-"), (3, "+")):
+                    added = (d == 1) == (e < 2)
+                    at = 256 * "AB".index(p) + 128 * (d // 2) + HALF * e
+                    rows = slice(at + low, at + high)
+                    needs = [txt_key(p, d, e)] + ([("t1", p, e, low)] if added else [])
+                    plan.work(
+                        ("t2 out", p, d, e, low), needs, 0.07, functools.partial(t2_out, p, d, e, low, high, added)
+                    )
+                    plan.copy(
+                        ("t2", p, d, e, low), [("t2 out", p, d, e, low)], QUART, t2_send.at[rows], t2_recv.at[rows],
+                        two + way, ("t2", p, e, low),
+                    )
+                if e:
+                    at = 96 * "AB".index(p) + HALF * (e - 1)
+                    rows = slice(at + low, at + high)
+                    plan.work(
+                        ("t3 out", p, e, low), line_needs(p, e, low), 0.08, functools.partial(t3_out, p, e, low, high)
+                    )
+                    plan.copy(
+                        ("t3", p, e, low), [("t3 out", p, e, low)], QUART, t3_send.at[rows], t3_recv.at[rows],
+                        one + " -2+"[e], ("t3", p),
+                    )
 
     def finish(embedding, total):
         unit, inverse = unit_rows(embedding)
@@ -410,9 +425,9 @@
     def finish_txt(p):
         low = HALF * "AB".index(p)
         total = line_sum(p, 0)
-        for side in halves:
-            at = OWN * "AB".index(p) + HALF * side
-            total = total + t4_recv[at:at + HALF, :].astype(f32)
+        for e in (1, 2, 3):
+            at = 96 * "AB".index(p) + HALF * (e - 1)
+            total = total + t3_recv[at:at + HALF, :].astype(f32)
         txt_out[low:low + HALF, :] = finish(txt_ref[low:low + HALF, :], total)
 
     def finish_img(low, high):
@@ -422,7 +437,7 @@
         img_out[low:high, :] = finish(img_ref[low:high, :], total)
 
     for p in "AB":
-        needs = line_needs(p, 0) + [("t4", p, side, part) for side in halves for part in halves]
+        needs = [need for low in (0, QUART) for need in line_needs(p, 0, low) + [("t3", p, e, low) for e in (1, 2, 3)]]
         plan.work(("end", p), needs, 0.2, functools.partial(finish_txt, p))
     for low in (HALF, 0):
         needs = [img_key(0, 0), ("s", 0), ("r", 1, low)]
@@ -439,7 +454,7 @@
 
     here = set()
     for key in plan.order()[0]:
-        needs, _, run, link, _ = plan.steps[key]
+        needs, _, run, links, _ = plan.steps[key]
         for need in needs:
             group = plan.group_of.get(need)
             if group is None or group in here:
@@ -448,7 +463,7 @@
             landed = [plan.steps[member][2][1] for member in plan.groups[group]]
             ids = landed[0].dtype != bf16
             await_copy(whole(sum(1 if ref.ndim == 2 and ids else ref.shape[0] for ref in landed), ids), arrives[group])
-        if link is None:
+        if links is None:
             run()
             continue
         src, dst, to = run
@@ -508,10 +523,8 @@
             pltpu.VMEM((256, D), bf16),
             pltpu.VMEM((512, D), bf16),
             pltpu.VMEM((512, D), bf16),
-            pltpu.VMEM((64, D), bf16),
-            pltpu.VMEM((64, D), bf16),
-            pltpu.VMEM((128, D), bf16),
-            pltpu.VMEM((128, D), bf16),
+            pltpu.VMEM((192, D), bf16),
+            pltpu.VMEM((192, D), bf16),
             pltpu.VMEM((512, D), bf16),
             pltpu.VMEM((512, D), bf16),
             pltpu.VMEM((512, D), bf16),

time: 52.2 us -> 50.9 us (0.975)
  Pallas kernels: 50 us -> 48.5 us
    pallas_call x1, Pallas kernels: 49.1 us -> 47.7 us  [body(): pl.pallas_call(kernel, out_shape=(pltpu.VMEM((OWN, D), f32), pltpu.VMEM((...]
where the time goes in v1:
time: 50.9 us; the launch traced here: 50.4 us
  Pallas kernels  48.5 us (95%)
  between operations  1.93 us (4%)
    pallas_call x1, Pallas kernels, body(): pl.pallas_call(kernel, out_shape=(pltpu.VMEM((OWN, D), f32), pltpu.VMEM((...  47.7 us

profile of v1, /device:TPU:1, one launch (start us, length us, event | category | flops | bytes accessed | tf_op | source)
XLA Modules:
  0.0 50.4 jit_solution(1390631438364412929)
XLA Ops:
  1.9 47.7 %shard_map.77 = (f32[64,1152]{1,0:T(8,128)S(1)}, f32[64,1152]{1,0:T(8,128)S(1)}) custom-call(bf16[64,1152]{1,0:T(8,128)(2,1)} %img_in.1, bf16[64,1152]{1,0:T(8,128)(2,1)} %txt_in.1, s32[1,64]{1,0:T(1,128)} %bitcast.6, s32[1,64]{1,0:T(1,128)} %bitcast.7, f32[1,1]{1,0:T(1,128)} %bitcast.4.scale_in, f32[1,1]{1,0:T(1,128)} %bitcast.5.bias_in), custom_call_target="tpu_custom_call" | custom-call | flops 7247757312 | bytes 900000 | tf_op jit(solution)/shard_map/pallas_call | solution.py:500
  49.6 0.8 %shard_map.78 = (f32[64,1152]{1,0:T(8,128)}, f32[64,1152]{1,0:T(8,128)}) custom-call(f32[64,1152]{1,0:T(8,128)S(1)} %get-tuple-element.4.img_grad, f32[64,1152]{1,0:T(8,128)S(1)} %get-tuple-element.5.txt_grad), custom_call_target="tpu_custom_call" | custom-call | tf_op jit(solution)/shard_map/pallas_call | solution.py:541

commit v2 on v1

--- a/solution.py
+++ b/solution.py
@@ -17,7 +17,7 @@
 N_ARRIVALS = 146
 N_SENT = 6
 
-LINK_ROW, CORE_ROW, LINK_WAIT, CORE_WAIT, ISSUE, QUEUE = 0.0493, 0.0035, 2.2, 1.7, 0.03, 1.6
+LINK_ROW, CORE_ROW, LINK_WAIT, CORE_WAIT, ISSUE, QUEUE = 0.0493, 0.0035, 2.4, 2.4, 0.02, 1.6
 ROUTE = {
     **{way: ((way,), 1, 0.0) for way in ("x+", "x-", "y+", "y-", "z+", "z-", "core")},
     "x2": (("x+", "x-"), 1, 0.6), "y2": (("y+", "y-"), 1, 0.6), "z+2": (("z+",), 2, 0.6), "z-2": (("z-",), 2, 0.6),
@@ -297,7 +297,7 @@
             needs += [at for piece in halves for at in text_here(p, d, e, piece)]
         key = ("score", r, high, t, right)
         score_keys.append(key)
-        cost = 0.12 + max(0.225, 0.00088 * (high - r)) * (right - t) / 256
+        cost = 0.08 + max(0.15, 0.0006 * (high - r)) * (right - t) / 256
         plan.work(key, needs, cost, functools.partial(score_tile, r, high, t, right))
 
     def img_terms(row):
@@ -310,9 +310,9 @@
 
     for row in range(0, ROWS, 128):
         needs = [key for key in score_keys if key[1] <= row < key[2]]
-        plan.work(("img", row), needs, 0.37, functools.partial(img_terms, row))
+        plan.work(("img", row), needs, 0.41, functools.partial(img_terms, row))
         needs = [key for key in score_keys if key[3] <= row < key[4]]
-        plan.work(("txt", row), needs, 0.38, functools.partial(txt_terms, row))
+        plan.work(("txt", row), needs, 0.42, functools.partial(txt_terms, row))
 
     def img_key(dz, cr):
         return ("img", IMG_ROW[dz, cr] // 128 * 128)
@@ -333,7 +333,7 @@
 
     for dz in range(8):
         rows = slice(OWN * dz, OWN * dz + OWN)
-        plan.work(("to core", dz), [img_key(dz, 1)], 0.12, functools.partial(to_core, dz))
+        plan.work(("to core", dz), [img_key(dz, 1)], 0.04, functools.partial(to_core, dz))
         plan.copy(("s", dz), [("to core", dz)], OWN, core_send.at[rows], core_recv.at[rows], "core", ("s", min(dz, 8 - dz)))
     for dz in (4, 3, 5, 2, 6, 1, 7):
         for low, high in pieces:
@@ -344,7 +344,7 @@
             if dz in (2, 6) and (low < HALF) == (dz == 2):
                 before.append(4)
             needs = [img_key(dz, 0), ("s", dz)] + [("r", other, low) for other in before]
-            plan.work(("z out", dz, low), needs, 0.08, functools.partial(z_out, dz, low, high, before))
+            plan.work(("z out", dz, low), needs, 0.03, functools.partial(z_out, dz, low, high, before))
             rows = slice(OWN * dz + low, OWN * dz + high)
             plan.copy(
                 ("r", dz, low), [("z out", dz, low)], high - low, z_send.at[rows], z_recv.at[rows],
@@ -389,7 +389,7 @@
                 high = low + QUART
                 at = 128 * "AB".index(p) + HALF * e
                 rows = slice(at + low, at + high)
-                plan.work(("t1 out", p, e, low), [txt_key(p, 2, e)], 0.06, functools.partial(t1_out, p, e, low, high))
+                plan.work(("t1 out", p, e, low), [txt_key(p, 2, e)], 0.02, functools.partial(t1_out, p, e, low, high))
                 plan.copy(
                     ("t1", p, e, low), [("t1 out", p, e, low)], QUART, t1_send.at[rows], t1_recv.at[rows],
                     two + ("-" if e < 2 else "+"),
@@ -400,7 +400,7 @@
                     rows = slice(at + low, at + high)
                     needs = [txt_key(p, d, e)] + ([("t1", p, e, low)] if added else [])
                     plan.work(
-                        ("t2 out", p, d, e, low), needs, 0.07, functools.partial(t2_out, p, d, e, low, high, added)
+                        ("t2 out", p, d, e, low), needs, 0.03, functools.partial(t2_out, p, d, e, low, high, added)
                     )
                     plan.copy(
                         ("t2", p, d, e, low), [("t2 out", p, d, e, low)], QUART, t2_send.at[rows], t2_recv.at[rows],
@@ -410,7 +410,7 @@
                     at = 96 * "AB".index(p) + HALF * (e - 1)
                     rows = slice(at + low, at + high)
                     plan.work(
-                        ("t3 out", p, e, low), line_needs(p, e, low), 0.08, functools.partial(t3_out, p, e, low, high)
+                        ("t3 out", p, e, low), line_needs(p, e, low), 0.03, functools.partial(t3_out, p, e, low, high)
                     )
                     plan.copy(
                         ("t3", p, e, low), [("t3 out", p, e, low)], QUART, t3_send.at[rows], t3_recv.at[rows],

time: 50.9 us -> 50.1 us (0.984)
  Pallas kernels: 48.5 us -> 47.5 us
    pallas_call x1, Pallas kernels: 47.7 us -> 46.7 us  [body(): pl.pallas_call(kernel, out_shape=(pltpu.VMEM((OWN, D), f32), pltpu.VMEM((...]
where the time goes in v2:
time: 50.1 us; the launch traced here: 49.4 us
  Pallas kernels  47.5 us (95%)
  between operations  1.93 us (4%)
    pallas_call x1, Pallas kernels, body(): pl.pallas_call(kernel, out_shape=(pltpu.VMEM((OWN, D), f32), pltpu.VMEM((...  46.7 us

profile of v2, /device:TPU:1, one launch (start us, length us, event | category | flops | bytes accessed | tf_op | source)
XLA Modules:
  0.0 49.4 jit_solution(649916707814270766)
XLA Ops:
  1.9 46.7 %shard_map.77 = (f32[64,1152]{1,0:T(8,128)S(1)}, f32[64,1152]{1,0:T(8,128)S(1)}) custom-call(bf16[64,1152]{1,0:T(8,128)(2,1)} %img_in.1, bf16[64,1152]{1,0:T(8,128)(2,1)} %txt_in.1, s32[1,64]{1,0:T(1,128)} %bitcast.6, s32[1,64]{1,0:T(1,128)} %bitcast.7, f32[1,1]{1,0:T(1,128)} %bitcast.4.scale_in, f32[1,1]{1,0:T(1,128)} %bitcast.5.bias_in), custom_call_target="tpu_custom_call" | custom-call | flops 7247757312 | bytes 900000 | tf_op jit(solution)/shard_map/pallas_call | solution.py:500
  48.6 0.8 %shard_map.78 = (f32[64,1152]{1,0:T(8,128)}, f32[64,1152]{1,0:T(8,128)}) custom-call(f32[64,1152]{1,0:T(8,128)S(1)} %get-tuple-element.4.img_grad, f32[64,1152]{1,0:T(8,128)S(1)} %get-tuple-element.5.txt_grad), custom_call_target="tpu_custom_call" | custom-call | tf_op jit(solution)/shard_map/pallas_call | solution.py:541

commit v3 on v2

--- a/solution.py
+++ b/solution.py
@@ -484,8 +484,9 @@
 
 def write_out(img_grad, txt_grad, img_out, txt_out, sems):
     copies = [
-        pltpu.make_async_copy(src, dst, sems.at[number])
-        for number, (src, dst) in enumerate([(img_grad, img_out), (txt_grad, txt_out)])
+        pltpu.make_async_copy(src.at[low:low + QUART], dst.at[low:low + QUART], sems.at[side, low // QUART])
+        for low in range(0, OWN, QUART)
+        for side, (src, dst) in enumerate([(img_grad, img_out), (txt_grad, txt_out)])
     ]
     for copy in copies:
         copy.start()
@@ -543,7 +544,7 @@
         out_shape=(jax.ShapeDtypeStruct((OWN, D), f32), jax.ShapeDtypeStruct((OWN, D), f32)),
         in_specs=[in_vmem, in_vmem],
         out_specs=(anywhere, anywhere),
-        scratch_shapes=[pltpu.SemaphoreType.DMA((2,))],
+        scratch_shapes=[pltpu.SemaphoreType.DMA((2, OWN // QUART))],
     )(*[pltpu.with_memory_space_constraint(grad, pltpu.VMEM) for grad in grads])
 
 

time: 50.1 us -> 50.2 us (level)
  no operation moved by 1% of the time
where the time goes in v3:
time: 50.2 us; the launch traced here: 49.5 us
  Pallas kernels  47.5 us (95%)
  between operations  1.93 us (4%)
    pallas_call x1, Pallas kernels, body(): pl.pallas_call(kernel, out_shape=(pltpu.VMEM((OWN, D), f32), pltpu.VMEM((...  46.7 us

profile of v3, /device:TPU:1, one launch (start us, length us, event | category | flops | bytes accessed | tf_op | source)
XLA Modules:
  0.0 49.5 jit_solution(2089930858072847097)
XLA Ops:
  1.9 46.7 %shard_map.77 = (f32[64,1152]{1,0:T(8,128)S(1)}, f32[64,1152]{1,0:T(8,128)S(1)}) custom-call(bf16[64,1152]{1,0:T(8,128)(2,1)} %img_in.1, bf16[64,1152]{1,0:T(8,128)(2,1)} %txt_in.1, s32[1,64]{1,0:T(1,128)} %bitcast.6, s32[1,64]{1,0:T(1,128)} %bitcast.7, f32[1,1]{1,0:T(1,128)} %bitcast.4.scale_in, f32[1,1]{1,0:T(1,128)} %bitcast.5.bias_in), custom_call_target="tpu_custom_call" | custom-call | flops 7247757312 | bytes 900000 | tf_op jit(solution)/shard_map/pallas_call | solution.py:501
  48.6 0.9 %shard_map.78 = (f32[64,1152]{1,0:T(8,128)}, f32[64,1152]{1,0:T(8,128)}) custom-call(f32[64,1152]{1,0:T(8,128)S(1)} %get-tuple-element.4.img_grad, f32[64,1152]{1,0:T(8,128)S(1)} %get-tuple-element.5.txt_grad), custom_call_target="tpu_custom_call" | custom-call | tf_op jit(solution)/shard_map/pallas_call | solution.py:542
